TPU v7x, 512 devices: a whole 4x8x8 slice. The times are simulated.
512 devices in a mesh: orient: 16 (over y_hi, z), slab: 32 (over x, y_lo, core).
Axes of the slice: x: 4, y: 8 (y_hi: 2, y_lo: 4; y = y_hi * 4 + y_lo), z: 8, core: 2. Of those that a mesh axis runs over, the one named last changes fastest.
Arguments:
- images: bfloat16 [1024, 65536], P('orient', 'slab'), may hold values from -8 to 8
- projections: bfloat16 [8, 768, 65536], P(None, 'orient', 'slab'), may hold values from -0.0234375 to 0.0234375
- noise_weight: float32 [65536], P('slab'), may hold values from 0.5 to 4
- prior_score: float32 [8, 768], P(None, 'orient'), may hold values from -4 to 4
- routing: int32 [32, 768, 16, 2], P('slab', 'orient'), may hold values from 0 to 63, as said below
- insert_kernel: bfloat16 [32, 64, 128, 128], P('slab', 'orient'), may hold values from -1.5 to 1.5
Outputs:
- volume: float32 [32, 64, 8, 128], P('slab', 'orient')
Inputs may be any that keep to these rules, and one draw needn't show every extreme that they name: routing[s, o, p, 0] names the slab owner that receives slice block s * 16 + p of orientation o, and routing[s, o, p, 1] a volume block of that owner's slab, below 64. Among the 768 entries with one s and one aligned block of 48 orientations, no owner is named more than 48 times, and for each aligned block of orientations there is one owner (the same for every s) that is named exactly 48 times for each s.
All inputs are finite; a program needn't handle non-finite values.
Results may differ from a plain program's by a relative error of at most 0.008.
Values may be sent and summed in bfloat16 or wider, within the bound.
No kernel may reach another device: no remote copies, remote signals or barrier semaphores. Data moves between devices by JAX's collectives and lax.ppermute only.
A program may use at most 64 MiB of HBM per device.

v0:
```python
import jax
import jax.numpy as jnp
from jax import lax
from jax.sharding import PartitionSpec as P

PIECE = 128


def joined(value, axis, join):
    pieces = jax.tree.map(lambda part: lax.all_gather(part, axis), value)
    head = jax.tree.map(lambda part: part[0], pieces)
    tail = jax.tree.map(lambda part: part[1:], pieces)
    subtotal, _ = lax.scan(lambda subtotal, slab: (join(subtotal, slab), None), head, tail)
    return subtotal


def combine_totals(earlier, later):
    ceiling = jnp.maximum(earlier[0], later[0])
    return (
        ceiling,
        earlier[1] * jnp.exp(earlier[0] - ceiling) + later[1] * jnp.exp(later[0] - ceiling),
    )


def normalize(scores):
    row_ceiling = jnp.max(scores, axis=1)
    summed = jnp.sum(jnp.exp(scores - row_ceiling[:, None]), axis=1)
    ceiling_all, summed_all = joined((row_ceiling, summed), "orient", combine_totals)
    log_total = ceiling_all + jnp.log(summed_all)
    return jnp.exp(scores - log_total[:, None]).astype(jnp.bfloat16)


def local(images, projections, noise_weight, prior_score, routing, insert_kernel):
    classes, orient_local, pixels_local = projections.shape
    columns = classes * orient_local
    image_rows = images.shape[0]
    orient_count = lax.axis_size("orient")
    slab_count = lax.axis_size("slab")
    all_images = image_rows * orient_count
    widened = projections.astype(jnp.float32)
    weighted = (
        (widened * noise_weight[None, None, :]).astype(jnp.bfloat16).reshape(columns, pixels_local)
    )
    penalty = (-0.5 * jnp.sum(widened * widened * noise_weight[None, None, :], axis=2)).reshape(
        columns
    )
    block_rows = lax.all_gather(images, "orient", axis=0, tiled=True)
    block_scores = (
        lax.dot_general(
            block_rows, weighted, (((1,), (1,)), ((), ())), preferred_element_type=jnp.float32
        )
        + penalty[None, :]
    )
    partial_scores = block_scores
    stored = block_rows
    partial_scores, stored = (partial_scores, stored)
    prior_row = prior_score.reshape(columns)
    scores = lax.psum(partial_scores, "slab") + prior_row[None, :]
    weights = normalize(scores)
    block_count = pixels_local // PIECE
    weight_cube = weights.reshape(all_images, classes, orient_local)
    stored_blocks = stored.reshape(all_images, block_count, PIECE)
    slices = jnp.einsum(
        "iko,ipc->opkc", weight_cube, stored_blocks, preferred_element_type=jnp.float32
    ).astype(jnp.bfloat16)
    piece_count = orient_local * block_count
    slices = slices.reshape(piece_count, classes * PIECE)
    target = routing[0, :, :, 0].reshape(piece_count)
    voxel_index = routing[0, :, :, 1].reshape(piece_count)
    capacity = 2 * piece_count // slab_count
    owner_onehot = (target[:, None] == jnp.arange(slab_count, dtype=jnp.int32)[None, :]).astype(
        jnp.int32
    )
    before = jnp.cumsum(owner_onehot, axis=0) - owner_onehot
    slot_rank = jnp.sum(before * owner_onehot, axis=1)
    slot_index = target * capacity + slot_rank
    placing = (
        jnp.arange(slab_count * capacity, dtype=jnp.int32)[:, None] == slot_index[None, :]
    ).astype(jnp.int32)
    outgoing = jnp.dot(
        placing.astype(jnp.bfloat16), slices, preferred_element_type=jnp.float32
    ).astype(jnp.bfloat16)
    voxel_blocks = insert_kernel.shape[1] * orient_count
    filled = jnp.sum(placing, axis=1)
    slot_voxel = jnp.sum(placing * voxel_index[None, :], axis=1) + (1 - filled) * voxel_blocks
    arriving, arriving_voxel = (
        lax.all_to_all(
            outgoing.reshape(slab_count, capacity, classes * PIECE),
            "slab",
            split_axis=0,
            concat_axis=0,
            tiled=True,
        ),
        lax.all_to_all(
            slot_voxel.reshape(slab_count, capacity),
            "slab",
            split_axis=0,
            concat_axis=0,
            tiled=True,
        ),
    )
    received = arriving.reshape(slab_count * capacity, classes * PIECE)
    gathering = (
        jnp.arange(voxel_blocks, dtype=jnp.int32)[:, None]
        == arriving_voxel.reshape(slab_count * capacity)[None, :]
    ).astype(jnp.bfloat16)
    accumulated = jnp.dot(gathering, received, preferred_element_type=jnp.float32)
    own_blocks = lax.psum_scatter(accumulated, "orient", scatter_dimension=0, tiled=True)
    rounded = own_blocks.astype(jnp.bfloat16).reshape(own_blocks.shape[0], classes, PIECE)
    volume = jnp.einsum(
        "vkc,vce->vke", rounded, insert_kernel[0], preferred_element_type=jnp.float32
    )
    return volume[None]


def solution(mesh):
    placed = (
        P("orient", "slab"),
        P(None, "orient", "slab"),
        P("slab"),
        P(None, "orient"),
        P("slab", "orient", None, None),
        P("slab", "orient", None, None),
    )
    return jax.shard_map(
        local,
        mesh=mesh,
        in_specs=placed,
        out_specs=P("slab", "orient", None, None),
        check_vma=False,
    )
```

profile of v0, /device:TPU:6, one launch (start us, length us, event | category | flops | bytes accessed | tf_op | source)
XLA Modules:
  0.0 723.8 jit_solution(9435200211898309589)
XLA Ops:
  6.5 0.0 copy-start
  6.5 0.0 all-gather.4.cloned.1.call-start
  6.5 0.7 all-gather.4.cloned.1.call-update
  7.3 0.0 all-reduce.4.cloned.1.call-start
  7.3 2.0 fusion.2
  9.4 0.1 mul.88
  9.4 138.5 %all-gather.4.cloned.1.call-done = bf16[1024,2048]{1,0:T(8,128)(2,1)} async-done(((bf16[64,2048]{1,0:T(8,128)(2,1)}), bf16[1024,2048]{1,0:T(8,128)(2,1)}) %all-gather.4.cloned.1.call-update) | async-done | bytes 4194320 | tf_op jit(solution)/shard_map/all_gather | solution.py:47
  148.0 5.2 add_bitcast_fusion
  153.1 0.0 copy-start.2
  153.1 0.0 copy-start.3
  153.1 0.0 all-reduce.4.cloned.1.call-update
  153.1 0.7 copy-done.2
  153.9 0.1 copy.21
  153.9 0.1 eq.56
  154.0 0.1 reshape_squeeze.3
  154.1 1.7 reduce-window.6
  155.8 0.3 slice_reduce_fusion
  156.1 0.1 copy.24
  156.2 0.1 mul.77
  156.3 0.1 fusion.12
  156.4 1.4 convert_reduce_fusion
  157.8 0.7 add.57
  158.5 5.7 all-to-all-start
  164.2 0.0 copy-done.3
  164.2 0.1 add.61
  164.3 6.4 copy.25
  170.7 248.4 %all-reduce.4.cloned.1.call-done = f32[1024,384]{0,1:T(8,128)} async-done(((f32[1024,384]{0,1:T(8,128)}), f32[1024,384]{0,1:T(8,128)}) %all-reduce.4.cloned.1.call-update) | async-done | bytes 1572880 | tf_op jit(solution)/shard_map/psum | solution.py:58
  419.2 0.0 copy-start.1
  419.2 1.7 add_reduce_fusion
  420.9 0.2 copy-done.1
  421.0 0.3 exponential_reduce_fusion
  421.4 51.7 %all-gather.1 = f32[16384]{0:T(1024)S(1)} all-gather(f32[1024]{0:T(1024)S(1)} %exponential_reduce_fusion), channel_id=3, replica_groups=mesh['orient'=16,'slab'=32] {'orient'}, dimensions={0}, use_global_device_ids=true | all-gather | bytes 69632 | tf_op jit(solution)/shard_map/all_gather | solution.py:10
  473.1 45.5 %all-gather = f32[16384]{0:T(1024)S(1)} all-gather(f32[1024]{0:T(1024)S(1)} %add_reduce_fusion), channel_id=2, replica_groups=mesh['orient'=16,'slab'=32] {'orient'}, dimensions={0}, use_global_device_ids=true | all-gather | bytes 69632 | tf_op jit(solution)/shard_map/all_gather | solution.py:10
  518.6 0.8 while.12
  519.4 0.3 exponential_convert_fusion
  519.8 4.0 fusion.6
  523.8 1.0 copy.27
  524.8 3.9 convolution_convert_fusion
  528.7 0.0 all-to-all-done
  528.7 20.4 %all-to-all-start.1 = ((bf16[32,48,1024]{2,1,0:T(8,128)(2,1)}), bf16[32,48,1024]{2,1,0:T(8,128)(2,1)S(1)}, u32[]{:S(2)}, u32[]{:S(2)}) async-start(bf16[32,48,1024]{2,1,0:T(8,128)(2,1)} %bitcast.76), calls=%async_computation.1 | async-start | bytes 6291456 | tf_op jit(solution)/shard_map/all_to_all | solution.py:87
  549.2 1.3 dynamic-slice
  551.1 0.5 broadcast.61
  551.6 0.7 reduce.5
  552.3 0.1 eq.62
  552.4 67.7 %all-to-all-done.1 = bf16[32,48,1024]{2,1,0:T(8,128)(2,1)S(1)} async-done(((bf16[32,48,1024]{2,1,0:T(8,128)(2,1)}), bf16[32,48,1024]{2,1,0:T(8,128)(2,1)S(1)}, u32[]{:S(2)}, u32[]{:S(2)}) %all-to-all-start.1) | async-done | bytes 3145760 | tf_op jit(solution)/shard_map/all_to_all | solution.py:87
  620.1 0.7 fusion.7
  620.7 95.4 %all-reduce.5 = bf16[64,1024]{1,0:T(8,128)(2,1)S(1)} all-reduce(f32[64,1024]{1,0:T(8,128)S(1)} %fusion.7), channel_id=4, replica_groups=mesh['orient'=16,'slab'=32] {'orient'}, use_global_device_ids=true, to_apply=%region_11.12.clone | all-reduce | flops 65536 | bytes 393216
  716.2 0.0 copy-done
  716.2 0.8 convolution_bitcast_fusion
  (44 shorter events, 0.5 us)
Async XLA Ops:
  6.5 709.7 %copy-start = (bf16[1,4,128,128]{3,2,1,0:T(8,128)(2,1)S(1)}, bf16[1,4,128,128]{3,2,1,0:T(8,128)(2,1)}, u32[]{:S(2)}) copy-start(bf16[1,4,128,128]{3,2,1,0:T(8,128)(2,1)} %param.13) | copy-start | bytes 393220
  6.5 141.4 %all-gather.4.cloned.1.call-start = ((), (), s32[]{:S(2)}) async-start(), calls=%async_computation.2 | async-start | bytes 4456448 | tf_op jit(solution)/shard_map/all_gather | solution.py:47
  7.3 411.9 %all-reduce.4.cloned.1.call-start = ((), (), s32[]{:S(2)}) async-start(), calls=%async_computation.3 | async-start | bytes 3145728 | tf_op jit(solution)/shard_map/psum | solution.py:58
  153.1 0.7 copy-start.2
  153.1 11.1 %copy-start.3 = (f32[8,48]{1,0:T(8,128)S(1)}, f32[8,48]{1,0:T(8,128)}, u32[]{:S(2)}) copy-start(f32[8,48]{1,0:T(8,128)} %param.11) | copy-start | bytes 4612
  158.5 370.2 %all-to-all-start = ((s32[32,1,48]{2,1,0:T(1,128)}), s32[32,1,48]{2,1,0:T(1,128)S(1)}, u32[]{:S(2)}, u32[]{:S(2)}) async-start(s32[32,1,48]{2,1,0:T(1,128)} %add.57), calls=%async_computation | async-start | bytes 32768 | tf_op jit(solution)/shard_map/all_to_all | solution.py:94
  419.2 1.9 copy-start.1
  528.7 91.3 %all-to-all-start.1 = ((bf16[32,48,1024]{2,1,0:T(8,128)(2,1)}), bf16[32,48,1024]{2,1,0:T(8,128)(2,1)S(1)}, u32[]{:S(2)}, u32[]{:S(2)}) async-start(bf16[32,48,1024]{2,1,0:T(8,128)(2,1)} %bitcast.76), calls=%async_computation.1 | async-start | bytes 6291456 | tf_op jit(solution)/shard_map/all_to_all | solution.py:87
Sparse Core Ops, SparseCore 0:
  10.5 137.3 all-gather.3
  153.3 265.8 all-reduce.3
where the time goes:
time: 724 us
  waiting for transfers between devices  455 us (63%)
  blocking collectives  193 us (27%)
  starting transfers between devices  26.2 us (4%)
  matrix products  14.5 us (2%)
  between operations  14.2 us (2%)
  local copies, waits for them, and re-layouts  11.9 us (2%)
  other arithmetic  8.54 us (1%)
    psum x1, waiting for transfers between devices, local(): scores = lax.psum(partial_scores, 'slab') + prior_row[None, :]  248 us
    all_gather x1, waiting for transfers between devices, local(): block_rows = lax.all_gather(images, 'orient', axis=0, tiled=True)  139 us
    all_gather x2, blocking collectives, joined(): pieces = jax.tree.map(lambda part: lax.all_gather(part, axis), value)  97.2 us
    unnamed x1, blocking collectives  95.4 us
    all_to_all x1, waiting for transfers between devices, local(): lax.all_to_all(outgoing.reshape(slab_count, capacity, classes * PIECE), '...  67.7 us
    all_to_all x1, starting transfers between devices, local(): lax.all_to_all(outgoing.reshape(slab_count, capacity, classes * PIECE), '...  20.4 us
  transfers between devices with their start and end apart: 4, of which 3 were waited for; matrix products, arithmetic and copies ran while one was open for 4% of the time, Pallas kernels for 0%

commit v1 on v0

--- a/solution.py
+++ b/solution.py
@@ -4,6 +4,10 @@
 from jax.sharding import PartitionSpec as P
 
 PIECE = 128
+review_slots = lambda unit, at_axis: jnp.concatenate(
+    lax.all_to_all(jnp.stack([unit for _ in range(lax.axis_size("orient"))]), "orient", 0, 0),
+    axis=at_axis,
+)
 
 
 def joined(value, axis, join):
@@ -44,7 +48,7 @@
     penalty = (-0.5 * jnp.sum(widened * widened * noise_weight[None, None, :], axis=2)).reshape(
         columns
     )
-    block_rows = lax.all_gather(images, "orient", axis=0, tiled=True)
+    block_rows = review_slots(images, 0)
     block_scores = (
         lax.dot_general(
             block_rows, weighted, (((1,), (1,)), ((), ())), preferred_element_type=jnp.float32

time: 724 us -> 760 us (1.050)
  starting transfers between devices: 26.2 us -> 68.4 us
    all_gather x1 -> x0, waiting for transfers between devices: 139 us -> none  [local(): block_rows = lax.all_gather(images, 'orient', axis=0, tiled=True)]
    all_to_all x0 -> x1, waiting for transfers between devices: none -> 111 us  [lax.all_to_all(jnp.stack([unit for _ in range(lax.axis_size('orient'))]),...]
    all_to_all x1, starting transfers between devices: 5.7 us -> 32.1 us  [local(): lax.all_to_all(slot_voxel.reshape(slab_count, capacity), 'slab', split_ax...]
    psum x1, waiting for transfers between devices: 248 us -> 269 us  [local(): scores = lax.psum(partial_scores, 'slab') + prior_row[None, :]]
    all_to_all x0 -> x1, starting transfers between devices: none -> 15.9 us  [lax.all_to_all(jnp.stack([unit for _ in range(lax.axis_size('orient'))]),...]
  transfers between devices with their start and end apart: 4 -> 4, of which waited for: 3 -> 3; matrix products, arithmetic and copies ran while one was open for 4% -> 3% of each run, Pallas kernels for 0% -> 0%
where the time goes in v1:
time: 760 us; the launch traced here: 759 us
  waiting for transfers between devices  448 us (59%)
  blocking collectives  193 us (25%)
  starting transfers between devices  68.4 us (9%)
  local copies, waits for them, and re-layouts  14.5 us (2%)
  matrix products  14.5 us (2%)
  between operations  14.3 us (2%)
    psum x1, waiting for transfers between devices, local(): scores = lax.psum(partial_scores, 'slab') + prior_row[None, :]  269 us
    all_to_all x1, waiting for transfers between devices, lax.all_to_all(jnp.stack([unit for _ in range(lax.axis_size('orient'))]),...  111 us
    all_gather x2, blocking collectives, joined(): pieces = jax.tree.map(lambda part: lax.all_gather(part, axis), value)  97.2 us
    unnamed x1, blocking collectives  95.4 us
    all_to_all x1, waiting for transfers between devices, local(): lax.all_to_all(outgoing.reshape(slab_count, capacity, classes * PIECE), '...  67.7 us
    all_to_all x1, starting transfers between devices, local(): lax.all_to_all(slot_voxel.reshape(slab_count, capacity), 'slab', split_ax...  32.1 us
    all_to_all x1, starting transfers between devices, local(): lax.all_to_all(outgoing.reshape(slab_count, capacity, classes * PIECE), '...  20.4 us
    all_to_all x1, starting transfers between devices, lax.all_to_all(jnp.stack([unit for _ in range(lax.axis_size('orient'))]),...  15.9 us
  transfers between devices with their start and end apart: 4, of which 3 were waited for; matrix products, arithmetic and copies ran while one was open for 3% of the time, Pallas kernels for 0%

profile of v1, /device:TPU:6, one launch (start us, length us, event | category | flops | bytes accessed | tf_op | source)
XLA Modules:
  0.0 759.4 jit_solution(10104053410900078851)
XLA Ops:
  6.5 0.0 copy-start
  6.5 3.4 stack.2
  10.0 0.0 copy-start.2
  10.0 0.0 copy-start.4
  10.0 15.9 %all-to-all-start.1 = ((bf16[16,64,2048]{2,1,0:T(8,128)(2,1)}), bf16[16,64,2048]{2,1,0:T(8,128)(2,1)}, u32[]{:S(2)}, u32[]{:S(2)}) async-start(bf16[16,64,2048]{2,1,0:T(8,128)(2,1)} %stack.2), calls=%async_computation.1 | async-start | bytes 8388608 | tf_op jit(solution)/shard_map/all_to_all | solution.py:8
  25.8 0.0 all-reduce.4.cloned.1.call-start
  25.9 0.0 copy-done.2
  25.9 0.0 copy-done.4
  25.9 0.6 fusion.5
  26.6 0.1 mul.88
  26.6 111.0 %all-to-all-done.1 = bf16[16,64,2048]{2,1,0:T(8,128)(2,1)} async-done(((bf16[16,64,2048]{2,1,0:T(8,128)(2,1)}), bf16[16,64,2048]{2,1,0:T(8,128)(2,1)}, u32[]{:S(2)}, u32[]{:S(2)}) %all-to-all-start.1) | async-done | bytes 4194336 | tf_op jit(solution)/shard_map/all_to_all | solution.py:8
  137.7 5.2 add_bitcast_fusion
  142.8 0.0 copy-start.3
  142.8 0.0 copy-start.5
  142.8 0.0 all-reduce.4.cloned.1.call-update
  142.8 0.7 copy-done.3
  143.5 0.1 copy.19
  143.6 0.1 eq.56
  143.7 0.1 reshape_squeeze.3
  143.8 1.7 reduce-window.6
  145.5 0.3 slice_reduce_fusion
  145.8 0.1 copy.22
  145.9 0.1 mul.77
  146.0 0.1 fusion.20
  146.1 1.4 convert_reduce_fusion
  147.5 0.7 add.57
  148.2 32.1 %all-to-all-start = ((s32[32,1,48]{2,1,0:T(1,128)}), s32[32,1,48]{2,1,0:T(1,128)S(1)}, u32[]{:S(2)}, u32[]{:S(2)}) async-start(s32[32,1,48]{2,1,0:T(1,128)} %add.57), calls=%async_computation | async-start | bytes 32768 | tf_op jit(solution)/shard_map/all_to_all | solution.py:98
  180.3 0.0 copy-done.5
  180.3 0.1 add.61
  180.4 5.5 copy.27
  185.9 268.8 %all-reduce.4.cloned.1.call-done = f32[1024,384]{0,1:T(8,128)} async-done(((f32[1024,384]{0,1:T(8,128)}), f32[1024,384]{0,1:T(8,128)}) %all-reduce.4.cloned.1.call-update) | async-done | bytes 1572880 | tf_op jit(solution)/shard_map/psum | solution.py:62
  454.7 0.0 copy-start.1
  454.7 1.7 add_reduce_fusion
  456.4 0.2 copy-done.1
  456.6 0.3 exponential_reduce_fusion
  456.9 51.7 %all-gather.1 = f32[16384]{0:T(1024)S(1)} all-gather(f32[1024]{0:T(1024)S(1)} %exponential_reduce_fusion), channel_id=3, replica_groups=mesh['orient'=16,'slab'=32] {'orient'}, dimensions={0}, use_global_device_ids=true | all-gather | bytes 69632 | tf_op jit(solution)/shard_map/all_gather | solution.py:14
  508.6 45.5 %all-gather = f32[16384]{0:T(1024)S(1)} all-gather(f32[1024]{0:T(1024)S(1)} %add_reduce_fusion), channel_id=2, replica_groups=mesh['orient'=16,'slab'=32] {'orient'}, dimensions={0}, use_global_device_ids=true | all-gather | bytes 69632 | tf_op jit(solution)/shard_map/all_gather | solution.py:14
  554.2 0.8 while.12
  555.0 0.3 exponential_convert_fusion
  555.3 4.0 fusion.12
  559.3 1.0 copy.24
  560.3 3.9 convolution_convert_fusion
  564.3 0.0 all-to-all-done
  564.3 20.4 %all-to-all-start.2 = ((bf16[32,48,1024]{2,1,0:T(8,128)(2,1)}), bf16[32,48,1024]{2,1,0:T(8,128)(2,1)S(1)}, u32[]{:S(2)}, u32[]{:S(2)}) async-start(bf16[32,48,1024]{2,1,0:T(8,128)(2,1)} %bitcast.83), calls=%async_computation.2 | async-start | bytes 6291456 | tf_op jit(solution)/shard_map/all_to_all | solution.py:91
  584.7 1.3 dynamic-slice
  586.6 0.5 broadcast.63
  587.2 0.7 reduce.5
  587.9 0.1 eq.62
  587.9 67.7 %all-to-all-done.2 = bf16[32,48,1024]{2,1,0:T(8,128)(2,1)S(1)} async-done(((bf16[32,48,1024]{2,1,0:T(8,128)(2,1)}), bf16[32,48,1024]{2,1,0:T(8,128)(2,1)S(1)}, u32[]{:S(2)}, u32[]{:S(2)}) %all-to-all-start.2) | async-done | bytes 3145760 | tf_op jit(solution)/shard_map/all_to_all | solution.py:91
  655.6 0.7 fusion.15
  656.3 95.4 %all-reduce.5 = bf16[64,1024]{1,0:T(8,128)(2,1)S(1)} all-reduce(f32[64,1024]{1,0:T(8,128)S(1)} %fusion.15), channel_id=4, replica_groups=mesh['orient'=16,'slab'=32] {'orient'}, use_global_device_ids=true, to_apply=%region_11.12.clone | all-reduce | flops 65536 | bytes 393216
  751.7 0.0 copy-done
  751.8 0.8 convolution_bitcast_fusion
  (44 shorter events, 0.5 us)
Async XLA Ops:
  6.5 745.2 %copy-start = (bf16[1,4,128,128]{3,2,1,0:T(8,128)(2,1)S(1)}, bf16[1,4,128,128]{3,2,1,0:T(8,128)(2,1)}, u32[]{:S(2)}) copy-start(bf16[1,4,128,128]{3,2,1,0:T(8,128)(2,1)} %param.13) | copy-start | bytes 393220
  10.0 15.9 %copy-start.2 = (bf16[8,48,2048]{2,1,0:T(8,128)(2,1)S(1)}, bf16[8,48,2048]{2,1,0:T(8,128)(2,1)}, u32[]{:S(2)}) copy-start(bf16[8,48,2048]{2,1,0:T(8,128)(2,1)} %param.9) | copy-start | bytes 4718596
  10.0 15.9 %copy-start.4 = (f32[2048]{0:T(1024)S(1)}, f32[2048]{0:T(1024)}, u32[]{:S(2)}) copy-start(f32[2048]{0:T(1024)} %param.10) | copy-start | bytes 24580
  10.0 127.7 %all-to-all-start.1 = ((bf16[16,64,2048]{2,1,0:T(8,128)(2,1)}), bf16[16,64,2048]{2,1,0:T(8,128)(2,1)}, u32[]{:S(2)}, u32[]{:S(2)}) async-start(bf16[16,64,2048]{2,1,0:T(8,128)(2,1)} %stack.2), calls=%async_computation.1 | async-start | bytes 8388608 | tf_op jit(solution)/shard_map/all_to_all | solution.py:8
  25.8 428.9 %all-reduce.4.cloned.1.call-start = ((), (), s32[]{:S(2)}) async-start(), calls=%async_computation.3 | async-start | bytes 3145728 | tf_op jit(solution)/shard_map/psum | solution.py:62
  142.8 0.7 copy-start.3
  142.8 37.5 %copy-start.5 = (f32[8,48]{1,0:T(8,128)S(1)}, f32[8,48]{1,0:T(8,128)}, u32[]{:S(2)}) copy-start(f32[8,48]{1,0:T(8,128)} %param.11) | copy-start | bytes 4612
  148.2 416.1 %all-to-all-start = ((s32[32,1,48]{2,1,0:T(1,128)}), s32[32,1,48]{2,1,0:T(1,128)S(1)}, u32[]{:S(2)}, u32[]{:S(2)}) async-start(s32[32,1,48]{2,1,0:T(1,128)} %add.57), calls=%async_computation | async-start | bytes 32768 | tf_op jit(solution)/shard_map/all_to_all | solution.py:98
  454.7 1.9 copy-start.1
  564.3 91.3 %all-to-all-start.2 = ((bf16[32,48,1024]{2,1,0:T(8,128)(2,1)}), bf16[32,48,1024]{2,1,0:T(8,128)(2,1)S(1)}, u32[]{:S(2)}, u32[]{:S(2)}) async-start(bf16[32,48,1024]{2,1,0:T(8,128)(2,1)} %bitcast.83), calls=%async_computation.2 | async-start | bytes 6291456 | tf_op jit(solution)/shard_map/all_to_all | solution.py:91
Sparse Core Ops, SparseCore 0:
  143.0 311.7 all-reduce.3
